TPU v7x, 256 devices: a whole 4x4x8 slice. The times are simulated.
256 devices in a mesh: row: 8 (over y_hi, x), col: 16 (over z, y_lo), sea: 2 (over core).
Axes of the slice: x: 4, y: 4 (y_hi: 2, y_lo: 2; y = y_hi * 2 + y_lo), z: 8, core: 2. Of those that a mesh axis runs over, the one named last changes fastest.
Arguments:
- kernel: bfloat16 [16, 8, 768, 6144], P(None, None, 'col', 'row'), may hold values from -0.01953125 to 0.01953125
- history: bfloat16 [15, 8, 768, 512], P(None, None, 'col', 'sea'), may hold values from -6 to 6
- displacement: float32 [6144, 512], P(('row', 'col'), 'sea'), may hold values from -6 to 6
- velocity: float32 [6144, 512], P(('row', 'col'), 'sea'), may hold values from -6 to 6
- acceleration: float32 [6144, 512], P(('row', 'col'), 'sea'), may hold values from -6 to 6
- excitation: float32 [3, 6144, 512], P(None, ('row', 'col'), 'sea'), may hold values from -6 to 6
- solve_inverse: float32 [1024, 6, 6], P(('row', 'col')), may hold values from -2.5 to 2.5
- stiffness: float32 [1024, 6, 6], P(('row', 'col')), may hold values from -2.5 to 2.5
- owned: int32 [1024], replicated, may hold values from 0 to 1023, as said below
- links: int32 [1024, 16], P(('row', 'col')), may hold values from 0 to 16383, as said below
- arms: float32 [1024, 3, 16], P(('row', 'col')), may hold values from -1 to 1
Outputs:
- final_velocity: float32 [6144, 512], P(('row', 'col'), 'sea')
- deck_gaps: float32 [1024, 16, 3, 512], P(('row', 'col'), None, None, 'sea')
Inputs may be any that keep to these rules, and one draw needn't show every extreme that they name: `owned`: A permutation of the 1024 modules. Module m has its modes on the grid device m // 8 (row-major over row, col); its owner has the same col. The modules that one device sends to one owner number at most 2, exactly 2 wherever any are sent, and their list positions differ modulo 2. `links`: the partner point lies on another module listed to the same owner.
All inputs are finite; a program needn't handle non-finite values.
Results may differ from a plain program's by a relative error of at most 0.00037.
Values may be sent and summed in bfloat16 or wider, within the bound.
A program may use at most 128 MiB of HBM per device.

v0:
```python
import jax
import jax.numpy as jnp
from jax import lax
from jax.sharding import PartitionSpec as P

POINTS = 16
STEPS = 3
DT = 0.5
QUARTER = DT * DT / 4.0


def blocks(matrix, vector):
    return jnp.einsum("mab,mbr->mar", matrix, vector, precision=lax.Precision.HIGHEST)


def newmark(
    displacement, velocity, acceleration, force_now, excitation_now, solve_inverse, stiffness
):
    block_shape = (displacement.shape[0] // 6, 6, displacement.shape[1])
    predicted = displacement + DT * velocity + QUARTER * acceleration
    load_total = (
        excitation_now
        - force_now
        - blocks(stiffness, predicted.reshape(block_shape)).reshape(displacement.shape)
    )
    accel_next = blocks(solve_inverse, load_total.reshape(block_shape)).reshape(displacement.shape)
    return (
        predicted + QUARTER * accel_next,
        velocity + 0.5 * DT * (acceleration + accel_next),
        accel_next,
    )


def deck_motion(motion, levers):
    moving = motion[:, 0:3, None, :]
    turning = motion[:, 3:6, None, :]
    arm_all = levers[:, :, :, None]
    surge_motion = moving[:, 0] + turning[:, 1] * arm_all[:, 2] - turning[:, 2] * arm_all[:, 1]
    sway_motion = moving[:, 1] + turning[:, 2] * arm_all[:, 0] - turning[:, 0] * arm_all[:, 2]
    heave_motion = moving[:, 2] + turning[:, 0] * arm_all[:, 1] - turning[:, 1] * arm_all[:, 0]
    return jnp.stack([surge_motion, sway_motion, heave_motion], axis=2)


def body(
    kernel,
    history,
    displacement,
    velocity,
    acceleration,
    excitation,
    solve_inverse,
    stiffness,
    owned,
    links,
    arms,
):
    lag_count = kernel.shape[0]
    row_total = lax.axis_size("row")
    col_total = lax.axis_size("col")
    slab_rows = velocity.shape[0]
    block_rows = kernel.shape[3]
    module_count = slab_rows // 6
    window = history
    kernel_flat = kernel.reshape(-1, block_rows)
    for step_index in range(STEPS):
        newest = lax.all_gather(velocity.astype(jnp.bfloat16), "row", axis=0, tiled=True)
        newest = newest.reshape(1, row_total, slab_rows, newest.shape[1])
        window = jnp.concatenate([newest, window[: lag_count - 1]], axis=0)
        window_flat = window.reshape(kernel_flat.shape[0], -1)
        force_now = lax.psum_scatter(
            lax.dot_general(
                kernel_flat,
                window_flat,
                (((0,), (0,)), ((), ())),
                preferred_element_type=jnp.float32,
            ),
            "col",
            scatter_dimension=0,
            tiled=True,
        )
        displacement, velocity, acceleration = newmark(
            displacement,
            velocity,
            acceleration,
            force_now,
            excitation[step_index],
            solve_inverse,
            stiffness,
        )
    motion = displacement.reshape(module_count, 6, -1)
    grid_index = lax.axis_index("row") * col_total + lax.axis_index("col")
    owned_here = lax.dynamic_slice_in_dim(owned, grid_index * module_count, module_count, 0)
    home_rows = owned_here // (col_total * module_count)
    capacity = 2 * module_count // row_total
    local_ids = grid_index * module_count + jnp.arange(module_count, dtype=jnp.int32)
    list_range = jnp.arange(owned.shape[0], dtype=jnp.int32)
    positions = jnp.sum(
        jnp.where(owned[None, :] == local_ids[:, None], list_range[None, :], 0), axis=1
    )
    targets = (
        positions // (col_total * module_count) * capacity + positions % module_count % capacity
    )
    routing = (
        targets[None, :] == jnp.arange(row_total * capacity, dtype=jnp.int32)[:, None]
    ).astype(jnp.float32)
    outgoing = jnp.einsum("sm,mar->sar", routing, motion, precision=lax.Precision.HIGHEST).reshape(
        row_total, capacity, 6, -1
    )
    arrived = lax.all_to_all(outgoing, "row", split_axis=0, concat_axis=0, tiled=True).reshape(
        row_total * capacity, 6, -1
    )
    slot_index = jnp.arange(module_count, dtype=jnp.int32) % capacity
    owned_motion = jnp.take(arrived, home_rows * capacity + slot_index, axis=0)
    points = deck_motion(owned_motion, arms).reshape(module_count * POINTS, 3, -1)
    local_links = (links - grid_index * module_count * POINTS).reshape(-1)
    partner = jnp.take(points, local_links, axis=0)
    deck_gaps = (points - partner).reshape(module_count, POINTS, 3, -1)
    return (velocity, deck_gaps)


def solution(mesh):
    placed = (
        P(None, None, "col", "row"),
        P(None, None, "col", "sea"),
        P(("row", "col"), "sea"),
        P(("row", "col"), "sea"),
        P(("row", "col"), "sea"),
        P(None, ("row", "col"), "sea"),
        P(("row", "col"), None, None),
        P(("row", "col"), None, None),
        P(),
        P(("row", "col"), None),
        P(("row", "col"), None, None),
    )
    return jax.shard_map(
        body,
        mesh=mesh,
        in_specs=placed,
        out_specs=(P(("row", "col"), "sea"), P(("row", "col"), None, None, "sea")),
        check_vma=False,
    )
```

profile of v0, /device:TPU:2, one launch (start us, length us, event | category | flops | bytes accessed | tf_op | source)
XLA Modules:
  0.0 378.5 jit_solution(11167240367918859943)
XLA Ops:
  7.2 0.9 fusion.48
  8.1 34.6 %all_gather.9 = bf16[384,256]{1,0:T(8,128)(2,1)S(1)} all-gather(bf16[48,256]{1,0:T(8,128)(2,1)S(1)} %get-tuple-element.25), channel_id=1, replica_groups=mesh['row'=8,'col'=16,'sea'=2] {'row'}, dimensions={0}, use_global_device_ids=true | all-gather | bytes 221184 | tf_op jit(solution)/shard_map/all_gather | solution.py:66
  42.7 7.3 %fusion.14 = f32[768,256]{0,1:T(8,128)S(1)} fusion(bf16[16,8,48,768]{3,2,1,0:T(8,128)(2,1)} %param.11, bf16[15,8,48,256]{3,2,1,0:T(8,128)(2,1)} %param.12, bf16[1,8,48,256]{3,2,1,0:T(8,128)(2,1)S(1)} %bitcast.112), kind=kOutput, calls=%fused_computation.17 | convolution fusion | flops 2417491968 | bytes 13369344 | tf_op jit(solution)/shard_map/dot_general | solution.py:71
  50.0 1.2 copy.99
  51.5 73.3 %reduce-scatter.10.cloned.1.call-done = f32[48,256]{1,0:T(8,128)} async-done(((f32[768,256]{1,0:T(8,128)}), f32[48,256]{1,0:T(8,128)}) %reduce-scatter.10.cloned.1.call-update) | async-done | bytes 49168 | tf_op jit(solution)/shard_map/reduce_scatter | solution.py:70
  124.7 0.8 fusion.27
  125.8 34.0 %all_gather.10 = bf16[384,256]{1,0:T(8,128)(2,1)S(1)} all-gather(bf16[48,256]{1,0:T(8,128)(2,1)S(1)} %get-tuple-element.16), channel_id=1, replica_groups=mesh['row'=8,'col'=16,'sea'=2] {'row'}, dimensions={0}, use_global_device_ids=true | all-gather | bytes 221184 | tf_op jit(solution)/shard_map/all_gather | solution.py:66
  159.8 7.2 %fusion.17 = f32[768,256]{0,1:T(8,128)S(1)} fusion(bf16[16,8,48,768]{3,2,1,0:T(8,128)(2,1)} %param.11, bf16[15,8,48,256]{3,2,1,0:T(8,128)(2,1)} %param.12, bf16[1,8,48,256]{3,2,1,0:T(8,128)(2,1)S(1)} %bitcast.113, bf16[1,8,48,256]{3,2,1,0:T(8,128)(2,1)S(1)} %bitcast.115), kind=kOutput, calls=%fused_computation.18 | convolution fusion | flops 2419064832 | bytes 13565952 | tf_op jit(solution)/shard_map/dot_general | solution.py:71
  167.0 1.2 copy.101
  168.5 69.3 %reduce-scatter.12.cloned.1.call-done = f32[48,256]{1,0:T(8,128)} async-done(((f32[768,256]{1,0:T(8,128)}), f32[48,256]{1,0:T(8,128)}) %reduce-scatter.12.cloned.1.call-update) | async-done | bytes 49168 | tf_op jit(solution)/shard_map/reduce_scatter | solution.py:70
  237.7 0.8 fusion.26
  238.8 34.0 %all_gather.11 = bf16[384,256]{1,0:T(8,128)(2,1)S(1)} all-gather(bf16[48,256]{1,0:T(8,128)(2,1)S(1)} %get-tuple-element.14), channel_id=1, replica_groups=mesh['row'=8,'col'=16,'sea'=2] {'row'}, dimensions={0}, use_global_device_ids=true | all-gather | bytes 221184 | tf_op jit(solution)/shard_map/all_gather | solution.py:66
  272.8 7.1 %fusion.20 = f32[768,256]{0,1:T(8,128)S(1)} fusion(bf16[16,8,48,768]{3,2,1,0:T(8,128)(2,1)} %param.11, bf16[1,8,48,256]{3,2,1,0:T(8,128)(2,1)S(1)} %bitcast.116, bf16[15,8,48,256]{3,2,1,0:T(8,128)(2,1)} %param.12, bf16[1,8,48,256]{3,2,1,0:T(8,128)(2,1)S(1)} %bitcast.114, bf16[1,8,48,256]{3,2,1,0:T(8,128)(2,1)S(1)} %bitcast.117), kind=kOutput, calls=%fused_computation.19 | convolution fusion | flops 2420637696 | bytes 13762560 | tf_op jit(solution)/shard_map/dot_general | solution.py:71
  279.9 1.2 copy.103
  282.1 68.7 %reduce-scatter.14.cloned.1.call-done = f32[48,256]{1,0:T(8,128)} async-done(((f32[768,256]{1,0:T(8,128)}), f32[48,256]{1,0:T(8,128)}) %reduce-scatter.14.cloned.1.call-update) | async-done | bytes 49168 | tf_op jit(solution)/shard_map/reduce_scatter | solution.py:70
  350.8 0.8 fusion.25
  351.8 0.6 multiply_add_fusion
  352.7 0.7 copy.89
  353.4 7.0 %all-to-all-start = ((f32[8,2,6,256]{3,1,2,0:T(2,128)}), f32[8,2,6,256]{3,1,2,0:T(2,128)S(1)}, u32[]{:S(2)}, u32[]{:S(2)}) async-start(f32[8,2,6,256]{3,1,2,0:T(2,128)} %copy.89), calls=%async_computation | async-start | bytes 196608 | tf_op jit(solution)/shard_map/all_to_all | solution.py:109
  360.4 6.7 %all-to-all-done = f32[8,2,6,256]{3,1,2,0:T(2,128)S(1)} async-done(((f32[8,2,6,256]{3,1,2,0:T(2,128)}), f32[8,2,6,256]{3,1,2,0:T(2,128)S(1)}, u32[]{:S(2)}, u32[]{:S(2)}) %all-to-all-start) | async-done | bytes 98336 | tf_op jit(solution)/shard_map/all_to_all | solution.py:109
  367.1 0.6 gather_fusion
  368.8 0.7 multiply_subtract_fusion.2
  369.9 0.9 gather_fusion.1
  371.2 0.8 copy.93
  (85 shorter events, 4.0 us)
Async XLA Ops:
  7.2 44.1 %copy-start = (f32[8,6,6]{2,0,1:T(8,128)S(1)}, f32[8,6,6]{2,0,1:T(8,128)}, u32[]{:S(2)}) copy-start(f32[8,6,6]{2,0,1:T(8,128)} %param.18) | copy-start | bytes 3460
  7.2 117.5 %reduce-scatter.10.cloned.1.call-start = ((), (), s32[]{:S(2)}) async-start(), calls=%async_computation.4 | async-start | bytes 835584 | tf_op jit(solution)/shard_map/reduce_scatter | solution.py:70
  42.7 82.0 %copy-start.4 = (f32[3,48,256]{2,1,0:T(8,128)S(1)}, f32[3,48,256]{2,1,0:T(8,128)}, u32[]{:S(2)}) copy-start(f32[3,48,256]{2,1,0:T(8,128)} %param.16) | copy-start | bytes 442372
  42.7 82.9 %copy-start.3 = (f32[8,6,6]{2,0,1:T(8,128)S(1)}, f32[8,6,6]{2,0,1:T(8,128)}, u32[]{:S(2)}) copy-start(f32[8,6,6]{2,0,1:T(8,128)} %param.17) | copy-start | bytes 3460
  50.0 75.8 %copy-start.1 = (f32[48,256]{1,0:T(8,128)S(1)}, f32[48,256]{1,0:T(8,128)}, u32[]{:S(2)}) copy-start(f32[48,256]{1,0:T(8,128)} %param.14) | copy-start | bytes 147460
  50.0 75.8 %copy-start.2 = (f32[48,256]{1,0:T(8,128)S(1)}, f32[48,256]{1,0:T(8,128)}, u32[]{:S(2)}) copy-start(f32[48,256]{1,0:T(8,128)} %param.15) | copy-start | bytes 147460
  51.2 186.6 %reduce-scatter.12.cloned.1.call-start = ((), (), s32[]{:S(2)}) async-start(), calls=%async_computation.5 | async-start | bytes 835584 | tf_op jit(solution)/shard_map/reduce_scatter | solution.py:70
  159.8 8.4 %copy-start.5 = (f32[8,3,16]{2,0,1:T(8,128)S(1)}, f32[8,3,16]{2,0,1:T(8,128)}, u32[]{:S(2)}) copy-start(f32[8,3,16]{2,0,1:T(8,128)} %param.21) | copy-start | bytes 4612
  168.2 182.6 %reduce-scatter.14.cloned.1.call-start = ((), (), s32[]{:S(2)}) async-start(), calls=%async_computation.6 | async-start | bytes 835584 | tf_op jit(solution)/shard_map/reduce_scatter | solution.py:70
  272.8 8.3 %copy-start.7 = (s32[8,16]{1,0:T(8,128)S(1)}, s32[8,16]{1,0:T(8,128)}, u32[]{:S(2)}) copy-start(s32[8,16]{1,0:T(8,128)} %param.20) | copy-start | bytes 1540
  272.8 8.7 %copy-start.6 = (s32[1024]{0:T(1024)S(1)}, s32[1024]{0:T(1024)}, u32[]{:S(2)}) copy-start(s32[1024]{0:T(1024)} %param.19) | copy-start | bytes 12292
  353.4 13.7 %all-to-all-start = ((f32[8,2,6,256]{3,1,2,0:T(2,128)}), f32[8,2,6,256]{3,1,2,0:T(2,128)S(1)}, u32[]{:S(2)}, u32[]{:S(2)}) async-start(f32[8,2,6,256]{3,1,2,0:T(2,128)} %copy.89), calls=%async_computation | async-start | bytes 196608 | tf_op jit(solution)/shard_map/all_to_all | solution.py:109
Sparse Core Ops, SparseCore 0:
  51.3 73.3 reduce-scatter.9
  168.3 69.3 reduce-scatter.11
  281.2 69.4 reduce-scatter.13
where the time goes:
time: 379 us; the launch traced here: 378 us
  waiting for transfers between devices  218 us (58%)
  blocking collectives  103 us (27%)
  matrix products  22.9 us (6%)
  between operations  14.3 us (4%)
  local copies, waits for them, and re-layouts  7.9 us (2%)
  starting transfers between devices  7.09 us (2%)
  other arithmetic  5.75 us (2%)
    reduce_scatter x3, waiting for transfers between devices, body(): lax.psum_scatter(lax.dot_general(kernel_flat, window_flat, (((0,), (0,)),...  211 us
    all_gather x3, blocking collectives, body(): lax.all_gather(velocity.astype(jnp.bfloat16), 'row', axis=0, tiled=True)  103 us
    dot_general x3, matrix products, body(): lax.dot_general(kernel_flat, window_flat, (((0,), (0,)), ((), ())), prefe...  21.6 us
  transfers between devices with their start and end apart: 4, of which 4 were waited for; matrix products, arithmetic and copies ran while one was open for 0% of the time, Pallas kernels for 0%

commit v1 on v0

--- a/solution.py
+++ b/solution.py
@@ -63,7 +63,12 @@
     window = history
     kernel_flat = kernel.reshape(-1, block_rows)
     for step_index in range(STEPS):
-        newest = lax.all_gather(velocity.astype(jnp.bfloat16), "row", axis=0, tiled=True)
+        newest = jnp.concatenate(
+            lax.all_to_all(
+                jnp.stack([velocity.astype(jnp.bfloat16)] * lax.axis_size("row")), "row", 0, 0
+            ),
+            axis=0,
+        )
         newest = newest.reshape(1, row_total, slab_rows, newest.shape[1])
         window = jnp.concatenate([newest, window[: lag_count - 1]], axis=0)
         window_flat = window.reshape(kernel_flat.shape[0], -1)

time: 379 us -> 311 us (0.82)
  blocking collectives: 103 us -> 28.5 us
  starting transfers between devices: 7.09 us -> 14 us
    all_gather x3 -> x0, blocking collectives: 103 us -> none  [body(): lax.all_gather(velocity.astype(jnp.bfloat16), 'row', axis=0, tiled=True)]
    all_to_all x0 -> x2, blocking collectives: none -> 28.5 us  [body(): lax.all_to_all(jnp.stack([velocity.astype(jnp.bfloat16)] * lax.axis_size(...]
    reduce_scatter x3, waiting for transfers between devices: 211 us -> 202 us  [body(): lax.psum_scatter(lax.dot_general(kernel_flat, window_flat, (((0,), (0,)),...]
    all_to_all x0 -> x1, waiting for transfers between devices: none -> 7.25 us  [body(): lax.all_to_all(jnp.stack([velocity.astype(jnp.bfloat16)] * lax.axis_size(...]
    all_to_all x0 -> x1, starting transfers between devices: none -> 6.99 us  [body(): lax.all_to_all(jnp.stack([velocity.astype(jnp.bfloat16)] * lax.axis_size(...]
  transfers between devices with their start and end apart: 4 -> 5, of which waited for: 4 -> 5; matrix products, arithmetic and copies ran while one was open for 0% -> 0% of each run, Pallas kernels for 0% -> 0%
where the time goes in v1:
time: 311 us; the launch traced here: 310 us
  waiting for transfers between devices  216 us (69%)
  blocking collectives  28.5 us (9%)
  matrix products  22.9 us (7%)
  between operations  14.3 us (5%)
  starting transfers between devices  14 us (5%)
  local copies, waits for them, and re-layouts  8.59 us (3%)
  other arithmetic  5.72 us (2%)
    reduce_scatter x3, waiting for transfers between devices, body(): lax.psum_scatter(lax.dot_general(kernel_flat, window_flat, (((0,), (0,)),...  202 us
    all_to_all x2, blocking collectives, body(): lax.all_to_all(jnp.stack([velocity.astype(jnp.bfloat16)] * lax.axis_size(...  28.5 us
    dot_general x3, matrix products, body(): lax.dot_general(kernel_flat, window_flat, (((0,), (0,)), ((), ())), prefe...  21.5 us
    all_to_all x1, waiting for transfers between devices, body(): lax.all_to_all(jnp.stack([velocity.astype(jnp.bfloat16)] * lax.axis_size(...  7.25 us
    all_to_all x1, starting transfers between devices, body(): lax.all_to_all(jnp.stack([velocity.astype(jnp.bfloat16)] * lax.axis_size(...  6.99 us
    all_to_all x1, starting transfers between devices, body(): lax.all_to_all(outgoing, 'row', split_axis=0, concat_axis=0, tiled=True)  6.96 us
    all_to_all x1, waiting for transfers between devices, body(): lax.all_to_all(outgoing, 'row', split_axis=0, concat_axis=0, tiled=True)  6.74 us
  transfers between devices with their start and end apart: 5, of which 5 were waited for; matrix products, arithmetic and copies ran while one was open for 0% of the time, Pallas kernels for 0%

profile of v1, /device:TPU:2, one launch (start us, length us, event | category | flops | bytes accessed | tf_op | source)
XLA Modules:
  0.0 310.3 jit_solution(2728649367684105401)
XLA Ops:
  7.2 0.9 fusion.48
  8.1 14.5 %all_to_all.20 = bf16[8,48,256]{2,1,0:T(8,128)(2,1)S(1)} all-to-all(bf16[8,48,256]{2,1,0:T(8,128)(2,1)S(1)} %stack.10), channel_id=1, replica_groups=mesh['row'=8,'col'=16,'sea'=2] {'row'}, dimensions={0} | all-to-all | bytes 393216 | tf_op jit(solution)/shard_map/all_to_all | solution.py:67
  22.7 7.2 %fusion.14 = f32[768,256]{0,1:T(8,128)S(1)} fusion(bf16[16,8,48,768]{3,2,1,0:T(8,128)(2,1)} %param.11, bf16[15,8,48,256]{3,2,1,0:T(8,128)(2,1)} %param.12, bf16[1,8,48,256]{3,2,1,0:T(8,128)(2,1)S(1)} %bitcast.112), kind=kOutput, calls=%fused_computation.17 | convolution fusion | flops 2417491968 | bytes 13369344 | tf_op jit(solution)/shard_map/dot_general | solution.py:76
  29.9 1.2 copy.99
  31.4 70.3 %reduce-scatter.10.cloned.1.call-done = f32[48,256]{1,0:T(8,128)} async-done(((f32[768,256]{1,0:T(8,128)}), f32[48,256]{1,0:T(8,128)}) %reduce-scatter.10.cloned.1.call-update) | async-done | bytes 49168 | tf_op jit(solution)/shard_map/reduce_scatter | solution.py:75
  101.7 0.8 fusion.27
  102.8 13.9 %all_to_all.21 = bf16[8,48,256]{2,1,0:T(8,128)(2,1)S(1)} all-to-all(bf16[8,48,256]{2,1,0:T(8,128)(2,1)S(1)} %stack.11), channel_id=1, replica_groups=mesh['row'=8,'col'=16,'sea'=2] {'row'}, dimensions={0} | all-to-all | bytes 393216 | tf_op jit(solution)/shard_map/all_to_all | solution.py:67
  116.8 7.2 %fusion.17 = f32[768,256]{0,1:T(8,128)S(1)} fusion(bf16[16,8,48,768]{3,2,1,0:T(8,128)(2,1)} %param.11, bf16[15,8,48,256]{3,2,1,0:T(8,128)(2,1)} %param.12, bf16[1,8,48,256]{3,2,1,0:T(8,128)(2,1)S(1)} %bitcast.113, bf16[1,8,48,256]{3,2,1,0:T(8,128)(2,1)S(1)} %bitcast.115), kind=kOutput, calls=%fused_computation.18 | convolution fusion | flops 2419064832 | bytes 13565952 | tf_op jit(solution)/shard_map/dot_general | solution.py:76
  123.9 1.2 copy.101
  125.3 66.3 %reduce-scatter.12.cloned.1.call-done = f32[48,256]{1,0:T(8,128)} async-done(((f32[768,256]{1,0:T(8,128)}), f32[48,256]{1,0:T(8,128)}) %reduce-scatter.12.cloned.1.call-update) | async-done | bytes 49168 | tf_op jit(solution)/shard_map/reduce_scatter | solution.py:75
  191.6 0.8 fusion.26
  192.7 0.7 stack.12
  193.4 7.0 %all-to-all-start.2 = ((bf16[8,48,256]{2,1,0:T(8,128)(2,1)}), bf16[8,48,256]{2,1,0:T(8,128)(2,1)S(1)}, u32[]{:S(2)}, u32[]{:S(2)}) async-start(bf16[8,48,256]{2,1,0:T(8,128)(2,1)} %stack.12), calls=%async_computation.2 | async-start | bytes 393216 | tf_op jit(solution)/shard_map/all_to_all | solution.py:67
  200.4 7.3 %all-to-all-done.2 = bf16[8,48,256]{2,1,0:T(8,128)(2,1)S(1)} async-done(((bf16[8,48,256]{2,1,0:T(8,128)(2,1)}), bf16[8,48,256]{2,1,0:T(8,128)(2,1)S(1)}, u32[]{:S(2)}, u32[]{:S(2)}) %all-to-all-start.2) | async-done | bytes 196640 | tf_op jit(solution)/shard_map/all_to_all | solution.py:67
  207.7 7.1 %fusion.20 = f32[768,256]{0,1:T(8,128)S(1)} fusion(bf16[16,8,48,768]{3,2,1,0:T(8,128)(2,1)} %param.11, bf16[1,8,48,256]{3,2,1,0:T(8,128)(2,1)S(1)} %bitcast.116, bf16[15,8,48,256]{3,2,1,0:T(8,128)(2,1)} %param.12, bf16[1,8,48,256]{3,2,1,0:T(8,128)(2,1)S(1)} %bitcast.114, bf16[1,8,48,256]{3,2,1,0:T(8,128)(2,1)S(1)} %bitcast.117), kind=kOutput, calls=%fused_computation.19 | convolution fusion | flops 2420637696 | bytes 13762560 | tf_op jit(solution)/shard_map/dot_general | solution.py:76
  214.8 1.2 copy.103
  216.9 65.7 %reduce-scatter.14.cloned.1.call-done = f32[48,256]{1,0:T(8,128)} async-done(((f32[768,256]{1,0:T(8,128)}), f32[48,256]{1,0:T(8,128)}) %reduce-scatter.14.cloned.1.call-update) | async-done | bytes 49168 | tf_op jit(solution)/shard_map/reduce_scatter | solution.py:75
  282.7 0.8 fusion.25
  284.6 0.7 copy.89
  285.3 7.0 %all-to-all-start.3 = ((f32[8,2,6,256]{3,1,2,0:T(2,128)}), f32[8,2,6,256]{3,1,2,0:T(2,128)S(1)}, u32[]{:S(2)}, u32[]{:S(2)}) async-start(f32[8,2,6,256]{3,1,2,0:T(2,128)} %copy.89), calls=%async_computation.3 | async-start | bytes 196608 | tf_op jit(solution)/shard_map/all_to_all | solution.py:114
  292.3 6.7 %all-to-all-done.3 = f32[8,2,6,256]{3,1,2,0:T(2,128)S(1)} async-done(((f32[8,2,6,256]{3,1,2,0:T(2,128)}), f32[8,2,6,256]{3,1,2,0:T(2,128)S(1)}, u32[]{:S(2)}, u32[]{:S(2)}) %all-to-all-start.3) | async-done | bytes 98336 | tf_op jit(solution)/shard_map/all_to_all | solution.py:114
  300.7 0.7 multiply_subtract_fusion.2
  301.8 0.9 gather_fusion.1
  303.0 0.8 copy.93
  (89 shorter events, 5.2 us)
Async XLA Ops:
  7.2 24.0 %copy-start = (f32[8,6,6]{2,0,1:T(8,128)S(1)}, f32[8,6,6]{2,0,1:T(8,128)}, u32[]{:S(2)}) copy-start(f32[8,6,6]{2,0,1:T(8,128)} %param.18) | copy-start | bytes 3460
  7.2 94.5 %reduce-scatter.10.cloned.1.call-start = ((), (), s32[]{:S(2)}) async-start(), calls=%async_computation.7 | async-start | bytes 835584 | tf_op jit(solution)/shard_map/reduce_scatter | solution.py:75
  22.7 79.0 %copy-start.4 = (f32[3,48,256]{2,1,0:T(8,128)S(1)}, f32[3,48,256]{2,1,0:T(8,128)}, u32[]{:S(2)}) copy-start(f32[3,48,256]{2,1,0:T(8,128)} %param.16) | copy-start | bytes 442372
  22.7 79.8 %copy-start.3 = (f32[8,6,6]{2,0,1:T(8,128)S(1)}, f32[8,6,6]{2,0,1:T(8,128)}, u32[]{:S(2)}) copy-start(f32[8,6,6]{2,0,1:T(8,128)} %param.17) | copy-start | bytes 3460
  29.9 72.8 %copy-start.1 = (f32[48,256]{1,0:T(8,128)S(1)}, f32[48,256]{1,0:T(8,128)}, u32[]{:S(2)}) copy-start(f32[48,256]{1,0:T(8,128)} %param.14) | copy-start | bytes 147460
  29.9 72.8 %copy-start.2 = (f32[48,256]{1,0:T(8,128)S(1)}, f32[48,256]{1,0:T(8,128)}, u32[]{:S(2)}) copy-start(f32[48,256]{1,0:T(8,128)} %param.15) | copy-start | bytes 147460
  31.1 160.5 %reduce-scatter.12.cloned.1.call-start = ((), (), s32[]{:S(2)}) async-start(), calls=%async_computation.8 | async-start | bytes 835584 | tf_op jit(solution)/shard_map/reduce_scatter | solution.py:75
  123.9 76.5 %copy-start.5 = (f32[8,3,16]{2,0,1:T(8,128)S(1)}, f32[8,3,16]{2,0,1:T(8,128)}, u32[]{:S(2)}) copy-start(f32[8,3,16]{2,0,1:T(8,128)} %param.21) | copy-start | bytes 4612
  193.4 14.3 %all-to-all-start.2 = ((bf16[8,48,256]{2,1,0:T(8,128)(2,1)}), bf16[8,48,256]{2,1,0:T(8,128)(2,1)S(1)}, u32[]{:S(2)}, u32[]{:S(2)}) async-start(bf16[8,48,256]{2,1,0:T(8,128)(2,1)} %stack.12), calls=%async_computation.2 | async-start | bytes 393216 | tf_op jit(solution)/shard_map/all_to_all | solution.py:67
  200.4 82.3 %reduce-scatter.14.cloned.1.call-start = ((), (), s32[]{:S(2)}) async-start(), calls=%async_computation.9 | async-start | bytes 835584 | tf_op jit(solution)/shard_map/reduce_scatter | solution.py:75
  207.7 8.3 %copy-start.7 = (s32[8,16]{1,0:T(8,128)S(1)}, s32[8,16]{1,0:T(8,128)}, u32[]{:S(2)}) copy-start(s32[8,16]{1,0:T(8,128)} %param.20) | copy-start | bytes 1540
  207.7 8.7 %copy-start.6 = (s32[1024]{0:T(1024)S(1)}, s32[1024]{0:T(1024)}, u32[]{:S(2)}) copy-start(s32[1024]{0:T(1024)} %param.19) | copy-start | bytes 12292
  285.3 13.7 %all-to-all-start.3 = ((f32[8,2,6,256]{3,1,2,0:T(2,128)}), f32[8,2,6,256]{3,1,2,0:T(2,128)S(1)}, u32[]{:S(2)}, u32[]{:S(2)}) async-start(f32[8,2,6,256]{3,1,2,0:T(2,128)} %copy.89), calls=%async_computation.3 | async-start | bytes 196608 | tf_op jit(solution)/shard_map/all_to_all | solution.py:114
Sparse Core Ops, SparseCore 0:
  31.2 70.3 reduce-scatter.9
  125.2 66.3 reduce-scatter.11
  216.1 66.5 reduce-scatter.13
